TPU v7x, 32 devices: a whole 2x2x4 slice. The times are simulated.
32 devices in a mesh: row: 4 (over z), col: 4 (over y, x), rep: 2 (over core).
Axes of the slice: x: 2, y: 2, z: 4, core: 2. Of those that a mesh axis runs over, the one named last changes fastest.
Arguments:
- tokens: bfloat16 [128, 4096], P(('col', 'rep'), 'row'), may hold values from -6 to 6
- grad_out: bfloat16 [128, 4096], P(('col', 'rep'), 'row'), may hold values from -2.5 to 2.5
- gate_weight: bfloat16 [4096, 14336], P('row', 'col'), may hold values from -0.09375 to 0.09375
- up_weight: bfloat16 [4096, 14336], P('row', 'col'), may hold values from -0.09375 to 0.09375
- down_weight: bfloat16 [14336, 4096], P('col', 'row'), may hold values from -0.046875 to 0.046875
- gate_keep: int32 [32, 112], P('row', 'col'), may hold values from 0 to 1, as said below
- up_keep: int32 [32, 112], P('row', 'col'), may hold values from 0 to 1, as said below
- down_keep: int32 [112, 32], P('col', 'row'), may hold values from 0 to 1, as said below
Outputs:
- mixed: bfloat16 [128, 4096], P(('col', 'rep'), 'row')
- input_grad: bfloat16 [128, 4096], P(('col', 'rep'), 'row')
- gate_weight_grad: bfloat16 [4096, 14336], P('row', 'col')
- up_weight_grad: bfloat16 [4096, 14336], P('row', 'col')
- down_weight_grad: bfloat16 [14336, 4096], P('col', 'row')
Inputs may be any that keep to these rules, and one draw needn't show every extreme that they name: `gate_keep`: 1 keeps the 128 x 128 block of the gate projection, 0 prunes it; the kept share differs from one device's region to the next. `up_keep`: 1 keeps the 128 x 128 block of the up projection, 0 prunes it; the kept share differs from one device's region to the next. `down_keep`: 1 keeps the 128 x 128 block of the down projection, 0 prunes it; the kept share differs from one device's region to the next.
All inputs are finite; a program needn't handle non-finite values.
Results may differ from a plain program's by a relative error of at most 0.025.
Values may be sent and summed in bfloat16 or wider, within the bound.
A program may use at most 128 MiB of HBM per device.

v0:
```python
import jax
import jax.numpy as jnp
from jax import lax
from jax.sharding import PartitionSpec as P

PLAIN = (((1,), (0,)), ((), ()))
FLIPPED = (((1,), (1,)), ((), ()))
OVER_ROWS = (((0,), (0,)), ((), ()))


def masked(weight, keep):
    rows, cols = keep.shape
    tiled = weight.reshape(rows, weight.shape[0] // rows, cols, weight.shape[1] // cols)
    return (tiled * keep[:, None, :, None].astype(weight.dtype)).reshape(weight.shape)


def product(left, weight, flipped):
    return lax.dot_general(
        left, weight, FLIPPED if flipped else PLAIN, preferred_element_type=jnp.float32
    )


def swiglu_grads(back, gate_value, gate_sig, up_value):
    gate_grad = (back * up_value * gate_sig * (1.0 + gate_value * (1.0 - gate_sig))).astype(
        jnp.bfloat16
    )
    up_grad = (back * gate_value * gate_sig).astype(jnp.bfloat16)
    return (gate_grad, up_grad)


def per_device(
    tokens, grad_out, gate_weight, up_weight, down_weight, gate_keep, up_keep, down_keep
):
    model_block = tokens.shape[1]
    gate_used = masked(gate_weight, gate_keep)
    up_used = masked(up_weight, up_keep)
    down_used = masked(down_weight, down_keep)
    token_panel, grad_panel = (
        lax.all_gather(tokens, "col", axis=0, tiled=True),
        lax.all_gather(grad_out, "col", axis=0, tiled=True),
    )
    gate_part = product(token_panel, gate_used, False)
    up_part = product(token_panel, up_used, False)
    gate_sum, up_sum = (
        lax.psum(gate_part.astype(jnp.bfloat16), "row").astype(jnp.float32),
        lax.psum(up_part.astype(jnp.bfloat16), "row").astype(jnp.float32),
    )
    gate_sig = jax.nn.sigmoid(gate_sum)
    hidden = (gate_sum * gate_sig * up_sum).astype(jnp.bfloat16)
    back_part = product(grad_panel, down_used, True)
    back_sum = lax.psum(back_part.astype(jnp.bfloat16), "row").astype(jnp.float32)
    gate_grad, up_grad = swiglu_grads(back_sum, gate_sum, gate_sig, up_sum)
    gate_term = masked(
        lax.dot_general(token_panel, gate_grad, OVER_ROWS, preferred_element_type=jnp.float32),
        gate_keep,
    )
    up_term = masked(
        lax.dot_general(token_panel, up_grad, OVER_ROWS, preferred_element_type=jnp.float32),
        up_keep,
    )
    down_term = masked(
        lax.dot_general(hidden, grad_panel, OVER_ROWS, preferred_element_type=jnp.float32),
        down_keep,
    )
    gate_total, up_total, down_total = (
        lax.psum(gate_term.astype(jnp.bfloat16), "rep").astype(jnp.float32),
        lax.psum(up_term.astype(jnp.bfloat16), "rep").astype(jnp.float32),
        lax.psum(down_term.astype(jnp.bfloat16), "rep").astype(jnp.float32),
    )
    forward = product(hidden, down_used, False)
    backward = product(gate_grad, gate_used, True) + product(up_grad, up_used, True)
    combined = lax.psum_scatter(
        jnp.concatenate([forward, backward], axis=1).astype(jnp.bfloat16),
        "col",
        scatter_dimension=0,
        tiled=True,
    ).astype(jnp.float32)
    mixed = combined[:, :model_block].astype(jnp.bfloat16)
    input_grad = combined[:, model_block:].astype(jnp.bfloat16)
    return (
        mixed,
        input_grad,
        gate_total.astype(jnp.bfloat16),
        up_total.astype(jnp.bfloat16),
        down_total.astype(jnp.bfloat16),
    )


def solution(mesh):
    return jax.shard_map(
        per_device,
        mesh=mesh,
        in_specs=(
            P(("col", "rep"), "row"),
            P(("col", "rep"), "row"),
            P("row", "col"),
            P("row", "col"),
            P("col", "row"),
            P("row", "col"),
            P("row", "col"),
            P("col", "row"),
        ),
        out_specs=(
            P(("col", "rep"), "row"),
            P(("col", "rep"), "row"),
            P("row", "col"),
            P("row", "col"),
            P("col", "row"),
        ),
        check_vma=False,
    )
```

profile of v0, /device:TPU:0, one launch (start us, length us, event | category | flops | bytes accessed | tf_op | source)
XLA Modules:
  0.0 286.7 jit_solution(9862132662191601911)
XLA Ops:
  7.2 0.8 fusion.31
  8.0 0.8 fusion.30
  8.7 0.8 fusion.29
  9.8 10.1 %all_gather.6 = bf16[64,1024]{1,0:T(8,128)(2,1)S(1)} all-gather(bf16[16,1024]{1,0:T(8,128)(2,1)} %param.8), channel_id=1, replica_groups=mesh['row'=4,'col'=4,'rep'=2] {'col'}, dimensions={0}, use_global_device_ids=true | all-gather | bytes 163840 | tf_op jit(solution)/shard_map/all_gather | solution.py:39
  19.9 8.2 %all_gather.7 = bf16[64,1024]{1,0:T(8,128)(2,1)S(1)} all-gather(bf16[16,1024]{1,0:T(8,128)(2,1)} %param.9), channel_id=1, replica_groups=mesh['row'=4,'col'=4,'rep'=2] {'col'}, dimensions={0}, use_global_device_ids=true | all-gather | bytes 163840 | tf_op jit(solution)/shard_map/all_gather | solution.py:40
  28.2 10.4 %copy.20 = bf16[1024,3584]{0,1:T(8,128)(2,1)} copy(bf16[1024,3584]{1,0:T(8,128)(2,1)} %param.10) | data formatting | bytes 14680064 | tf_op args[2]
  38.6 10.4 %copy.22 = bf16[1024,3584]{0,1:T(8,128)(2,1)} copy(bf16[1024,3584]{1,0:T(8,128)(2,1)} %param.11) | data formatting | bytes 14680064 | tf_op args[3]
  48.9 1.0 mul.90
  50.0 9.1 %fusion.3 = bf16[64,3584]{1,0:T(8,128)(2,1)} fusion(bf16[64,1024]{1,0:T(8,128)(2,1)S(1)} %all_gather.6, bf16[1024,3584]{0,1:T(8,128)(2,1)} %copy.20, bf16[448,8,8,128]{3,2,1,0:T(8,128)(2,1)S(1)} %bitcast.75), kind=kOutput, calls=%fused_computation.12 | convolution fusion | flops 473661440 | bytes 15269888 | tf_op jit(solution)/shard_map/dot_general | solution.py:18
  59.1 1.0 mul.94
  60.2 3.3 %fusion.4 = bf16[64,3584]{1,0:T(8,128)(2,1)} fusion(bf16[64,1024]{1,0:T(8,128)(2,1)S(1)} %all_gather.6, bf16[1024,3584]{0,1:T(8,128)(2,1)S(1)} %bitcast.70, bf16[448,8,8,128]{3,2,1,0:T(8,128)(2,1)S(1)} %bitcast.77), kind=kOutput, calls=%fused_computation.13 | convolution fusion | flops 473661440 | bytes 15269888 | tf_op jit(solution)/shard_map/dot_general | solution.py:18
  63.5 1.0 mul.98
  64.5 3.0 %copy-done.2 = bf16[28,128,8,128]{3,2,1,0:T(8,128)(2,1)} copy-done((bf16[28,128,8,128]{3,2,1,0:T(8,128)(2,1)}, bf16[28,128,8,128]{3,2,1,0:T(8,128)(2,1)S(1)}, u32[]{:S(2)}) %copy-start.2) | copy-done | bytes 7340056
  67.5 6.2 %fusion.5 = bf16[64,3584]{1,0:T(8,128)(2,1)} fusion(bf16[64,1024]{1,0:T(8,128)(2,1)S(1)} %all_gather.7, bf16[3584,1024]{1,0:T(8,128)(2,1)} %param.12, bf16[448,8,8,128]{3,2,1,0:T(8,128)(2,1)S(1)} %bitcast.81), kind=kOutput, calls=%fused_computation.14 | convolution fusion | flops 473661440 | bytes 15269888 | tf_op jit(solution)/shard_map/dot_general | solution.py:18
  74.2 62.8 %all-reduce.5.cloned.1.call-done = (bf16[64,3584]{1,0:T(8,128)(2,1)}, bf16[64,3584]{1,0:T(8,128)(2,1)}, bf16[64,3584]{1,0:T(8,128)(2,1)}) async-done(((bf16[64,3584]{1,0:T(8,128)(2,1)}, bf16[64,3584]{1,0:T(8,128)(2,1)}, bf16[64,3584]{1,0:T(8,128)(2,1)}), (bf16[64,3584]{1,0:T(8,128)(2,1)}, bf16[64,3584]{1,0:T(8,128)(2,1)}, bf16[64,3584]{1,0:T(8,128)(2,1)})) %all-reduce.5.cloned.1.call-update) | async-done | bytes 1376272 | tf_op jit(solution)/shard_map/psum | solution.py:46
  137.0 7.5 %fusion.11 = bf16[64,1024]{1,0:T(8,128)(2,1)S(1)} fusion(bf16[3584,1024]{1,0:T(8,128)(2,1)} %param.12, bf16[448,8,8,128]{3,2,1,0:T(8,128)(2,1)} %bitcast.82, bf16[64,3584]{1,0:T(8,128)(2,1)} %get-tuple-element.15, bf16[64,3584]{1,0:T(8,128)(2,1)} %get-tuple-element.17), kind=kOutput, calls=%fused_computation.24 | convolution fusion | flops 475332608 | bytes 15728640 | tf_op jit(solution)/shard_map/dot_general | solution.py:18
  144.6 5.4 %fusion.6 = f32[64,1024]{1,0:T(8,128)S(1)} fusion(bf16[1024,3584]{0,1:T(8,128)(2,1)S(1)} %bitcast.74, bf16[448,8,8,128]{3,2,1,0:T(8,128)(2,1)} %bitcast.76, bf16[64,3584]{1,0:T(8,128)(2,1)S(1)} %copy-done.5, bf16[64,3584]{1,0:T(8,128)(2,1)S(1)} %copy-done.7, bf16[64,3584]{1,0:T(8,128)(2,1)S(1)} %copy-done.3), kind=kOutput, calls=%fused_computation.15 | convolution fusion | flops 476413952 | bytes 16318464 | tf_op jit(solution)/shard_map/dot_general | solution.py:18
  150.0 0.7 slice-done.7
  150.7 1.9 fusion.10
  152.5 0.7 pad_maximum_fusion
  153.4 1.0 mul.107
  154.6 5.1 %fusion.2 = bf16[1024,3584]{0,1:T(8,128)(2,1)} fusion(f32[448,8,8,128]{3,2,1,0:T(8,128)S(1)} %bitcast.68, bf16[64,1024]{1,0:T(8,128)(2,1)S(1)} %all_gather.6, bf16[64,3584]{1,0:T(8,128)(2,1)S(1)} %copy-done.6, bf16[64,3584]{1,0:T(8,128)(2,1)S(1)} %copy-done.8, bf16[64,3584]{1,0:T(8,128)(2,1)S(1)} %copy-done.4), kind=kOutput, calls=%fused_computation.5 | convolution fusion | flops 480083968 | bytes 23527424 | tf_op jit(solution)/shard_map/dot_general | solution.py:54
  159.6 1.0 mul.110
  160.7 5.1 %fusion.1 = bf16[1024,3584]{0,1:T(8,128)(2,1)} fusion(f32[448,8,8,128]{3,2,1,0:T(8,128)S(1)} %bitcast.67, bf16[64,1024]{1,0:T(8,128)(2,1)S(1)} %all_gather.6, bf16[64,3584]{1,0:T(8,128)(2,1)S(1)} %copy-done.4, bf16[64,3584]{1,0:T(8,128)(2,1)S(1)} %copy-done.8), kind=kOutput, calls=%fused_computation.3 | convolution fusion | flops 478937088 | bytes 23068672 | tf_op jit(solution)/shard_map/dot_general | solution.py:58
  165.8 1.0 mul.113
  166.8 5.1 %fusion = bf16[3584,1024]{1,0:T(8,128)(2,1)} fusion(f32[448,8,8,128]{3,2,1,0:T(8,128)S(1)} %bitcast.66, bf16[64,1024]{1,0:T(8,128)(2,1)S(1)} %all_gather.7, bf16[64,3584]{1,0:T(8,128)(2,1)S(1)} %copy-done.6, bf16[64,3584]{1,0:T(8,128)(2,1)S(1)} %copy-done.4), kind=kOutput, calls=%fused_computation.1 | convolution fusion | flops 478937088 | bytes 23068672 | tf_op jit(solution)/shard_map/dot_general | solution.py:62
  171.9 5.3 %reduce-scatter.2.cloned.1.call-done = bf16[16,2048]{1,0:T(8,128)(2,1)} async-done(((bf16[64,2048]{1,0:T(8,128)(2,1)}), bf16[16,2048]{1,0:T(8,128)(2,1)}) %reduce-scatter.2.cloned.1.call-update) | async-done | bytes 65552 | tf_op jit(solution)/shard_map/reduce_scatter | solution.py:72
  177.2 1.4 fusion.28
  178.6 74.8 %all-reduce.7.cloned.1.call-done = (bf16[1024,3584]{0,1:T(8,128)(2,1)}, bf16[1024,3584]{0,1:T(8,128)(2,1)}, bf16[3584,1024]{1,0:T(8,128)(2,1)}) async-done(((bf16[1024,3584]{0,1:T(8,128)(2,1)}, bf16[1024,3584]{0,1:T(8,128)(2,1)}, bf16[3584,1024]{1,0:T(8,128)(2,1)}), (bf16[1024,3584]{0,1:T(8,128)(2,1)}, bf16[1024,3584]{0,1:T(8,128)(2,1)}, bf16[3584,1024]{1,0:T(8,128)(2,1)})) %all-reduce.7.cloned.1.call-update) | async-done | bytes 22020112 | tf_op jit(solution)/shard_map/psum | solution.py:66
  253.4 9.9 %copy.27 = bf16[1024,3584]{1,0:T(8,128)(2,1)} copy(bf16[1024,3584]{0,1:T(8,128)(2,1)} %get-tuple-element.18) | data formatting | bytes 14680064
  263.3 9.9 %copy.28 = bf16[1024,3584]{1,0:T(8,128)(2,1)} copy(bf16[1024,3584]{0,1:T(8,128)(2,1)} %get-tuple-element.19) | data formatting | bytes 14680064
  273.2 7.0 %copy.59 = bf16[3584,1024]{1,0:T(8,128)(2,1)} copy(bf16[3584,1024]{1,0:T(8,128)(2,1)} %get-tuple-element.33) | data formatting | bytes 14680064
  (48 shorter events, 1.2 us)
Async XLA Ops:
  7.2 129.8 %all-reduce.5.cloned.1.call-start = ((), (), s32[]{:S(2)}) async-start(), calls=%async_computation.2 | async-start | bytes 2752512 | tf_op jit(solution)/shard_map/psum | solution.py:46
  48.9 11.2 %slice-start = ((s8[7340032]{0:T(1024)(128)(4,1)}), s8[4194304]{0:T(1024)(128)(4,1)S(1)}, s32[]{:S(2)}) async-start(s8[7340032]{0:T(1024)(128)(4,1)} %bitcast.69), calls=%async_computation.4 | async-start | bytes 8388608
  50.0 9.1 %copy-start = (bf16[8,128,28,128]{1,0,3,2:T(8,128)(2,1)}, bf16[8,128,28,128]{1,0,3,2:T(8,128)(2,1)S(1)}, u32[]{:S(2)}) copy-start(bf16[8,128,28,128]{1,0,3,2:T(8,128)(2,1)S(1)} %mul.90) | copy-start | bytes 22020100
  50.0 10.2 %slice-start.1 = ((s8[7340032]{0:T(1024)(128)(4,1)}), s8[3145728]{0:T(1024)(128)(4,1)S(1)}, s32[]{:S(2)}) async-start(s8[7340032]{0:T(1024)(128)(4,1)} %bitcast.69), calls=%async_computation.5 | async-start | bytes 6291456
  60.1 3.4 %copy-start.1 = (bf16[8,128,28,128]{1,0,3,2:T(8,128)(2,1)}, bf16[8,128,28,128]{1,0,3,2:T(8,128)(2,1)S(1)}, u32[]{:S(2)}) copy-start(bf16[8,128,28,128]{1,0,3,2:T(8,128)(2,1)S(1)} %mul.94) | copy-start | bytes 22020100
  64.5 3.0 %copy-start.2 = (bf16[28,128,8,128]{3,2,1,0:T(8,128)(2,1)}, bf16[28,128,8,128]{3,2,1,0:T(8,128)(2,1)S(1)}, u32[]{:S(2)}) copy-start(bf16[28,128,8,128]{3,2,1,0:T(8,128)(2,1)S(1)} %mul.98) | copy-start | bytes 22020100
  73.7 70.8 %slice-start.4 = ((s8[7340032]{0:T(1024)(128)(4,1)}), s8[3145728]{0:T(1024)(128)(4,1)S(1)}, s32[]{:S(2)}) async-start(s8[7340032]{0:T(1024)(128)(4,1)} %bitcast.73), calls=%async_computation.8 | async-start | bytes 6291456
  73.7 103.5 %reduce-scatter.2.cloned.1.call-start = ((), (), s32[]{:S(2)}) async-start(), calls=%async_computation.1 | async-start | bytes 327680 | tf_op jit(solution)/shard_map/reduce_scatter | solution.py:72
  137.0 7.5 %slice-start.5 = ((s8[7340032]{0:T(1024)(128)(4,1)}), s8[4194304]{0:T(1024)(128)(4,1)S(1)}, s32[]{:S(2)}) async-start(s8[7340032]{0:T(1024)(128)(4,1)} %bitcast.73), calls=%async_computation.9 | async-start | bytes 8388608
  137.0 7.5 %copy-start.3 = (bf16[64,3584]{1,0:T(8,128)(2,1)S(1)}, bf16[64,3584]{1,0:T(8,128)(2,1)}, u32[]{:S(2)}) copy-start(bf16[64,3584]{1,0:T(8,128)(2,1)} %get-tuple-element.17) | copy-start | bytes 1376260
  137.0 7.5 %copy-start.5 = (bf16[64,3584]{1,0:T(8,128)(2,1)S(1)}, bf16[64,3584]{1,0:T(8,128)(2,1)}, u32[]{:S(2)}) copy-start(bf16[64,3584]{1,0:T(8,128)(2,1)} %get-tuple-element.15) | copy-start | bytes 1376260
  137.0 7.5 %copy-start.7 = (bf16[64,3584]{1,0:T(8,128)(2,1)S(1)}, bf16[64,3584]{1,0:T(8,128)(2,1)}, u32[]{:S(2)}) copy-start(bf16[64,3584]{1,0:T(8,128)(2,1)} %get-tuple-element.16) | copy-start | bytes 1376260
  137.0 13.0 %slice-start.2 = ((s8[7340032]{0:T(1024)(128)(4,1)}), s8[4194304]{0:T(1024)(128)(4,1)S(1)}, s32[]{:S(2)}) async-start(s8[7340032]{0:T(1024)(128)(4,1)} %bitcast.71), calls=%async_computation.6 | async-start | bytes 8388608
  137.0 13.0 %slice-start.6 = ((s8[7340032]{0:T(1024)(128)(4,1)}), s8[4194304]{0:T(1024)(128)(4,1)S(1)}, s32[]{:S(2)}) async-start(s8[7340032]{0:T(1024)(128)(4,1)} %bitcast.78), calls=%async_computation.10 | async-start | bytes 8388608
  144.5 5.5 %slice-start.3 = ((s8[7340032]{0:T(1024)(128)(4,1)}), s8[3145728]{0:T(1024)(128)(4,1)S(1)}, s32[]{:S(2)}) async-start(s8[7340032]{0:T(1024)(128)(4,1)} %bitcast.71), calls=%async_computation.7 | async-start | bytes 6291456
  144.6 6.1 %slice-start.7 = ((s8[7340032]{0:T(1024)(128)(4,1)}), s8[3145728]{0:T(1024)(128)(4,1)S(1)}, s32[]{:S(2)}) async-start(s8[7340032]{0:T(1024)(128)(4,1)} %bitcast.78), calls=%async_computation.11 | async-start | bytes 6291456
  153.3 1.1 copy-start.4
  153.3 1.1 copy-start.6
  153.3 1.3 copy-start.8
  153.3 100.1 %all-reduce.7.cloned.1.call-start = ((), (), s32[]{:S(2)}) async-start(), calls=%async_computation.3 | async-start | bytes 44040192 | tf_op jit(solution)/shard_map/psum | solution.py:66
Sparse Core Ops, SparseCore 0:
  73.8 63.0 all-reduce.4
  153.4 23.7 reduce-scatter.1
  180.5 72.7 all-reduce.6
where the time goes:
time: 288 us; the launch traced here: 287 us
  waiting for transfers between devices  143 us (50%)
  local copies, waits for them, and re-layouts  59.5 us (21%)
  matrix products  48.6 us (17%)
  blocking collectives  18.3 us (6%)
  between operations  14 us (5%)
  other arithmetic  3.04 us (1%)
    psum x1, waiting for transfers between devices, per_device(): lax.psum(gate_term.astype(jnp.bfloat16), 'rep').astype(jnp.float32)  74.8 us
    psum x1, waiting for transfers between devices, per_device(): lax.psum(up_part.astype(jnp.bfloat16), 'row').astype(jnp.float32)  62.8 us
    unnamed x39, local copies, waits for them, and re-layouts  51.5 us
    dot_general x6, matrix products, product(): lax.dot_general(left, weight, FLIPPED if flipped else PLAIN, preferred_el...  33.4 us
    all_gather x1, blocking collectives, per_device(): lax.all_gather(tokens, 'col', axis=0, tiled=True)  10.1 us
    all_gather x1, blocking collectives, per_device(): lax.all_gather(grad_out, 'col', axis=0, tiled=True)  8.24 us
    mul x6, local copies, waits for them, and re-layouts, masked(): tiled * keep[:, None, :, None].astype(weight.dtype)  6.05 us
  transfers between devices with their start and end apart: 3, of which 3 were waited for; matrix products, arithmetic and copies ran while one was open for 7% of the time, Pallas kernels for 0%

commit v1 on v0

v1 whole, which is shorter than its diff:
```python
import functools

import jax
import jax.numpy as jnp
from jax import lax
from jax.experimental import pallas as pl
from jax.experimental.pallas import tpu as pltpu
from jax.sharding import PartitionSpec as P

PLAIN = (((1,), (0,)), ((), ()))
FLIPPED = (((1,), (1,)), ((), ()))
OVER_ROWS = (((0,), (0,)), ((), ()))
MESH = pl.DeviceIdType.MESH
BLOCK = 128
F32 = jnp.float32
BF16 = jnp.bfloat16


def masked(weight, keep):
    rows, cols = keep.shape
    tiled = weight.reshape(rows, weight.shape[0] // rows, cols, weight.shape[1] // cols)
    return (tiled * keep[:, None, :, None].astype(weight.dtype)).reshape(weight.shape)


def product(left, weight, flipped):
    return lax.dot_general(
        left, weight, FLIPPED if flipped else PLAIN, preferred_element_type=F32
    )


def swiglu_grads(back, gate_value, gate_sig, up_value):
    gate_grad = (back * up_value * gate_sig * (1.0 + gate_value * (1.0 - gate_sig))).astype(BF16)
    up_grad = (back * gate_value * gate_sig).astype(BF16)
    return (gate_grad, up_grad)


def plain_device(
    tokens, grad_out, gate_weight, up_weight, down_weight, gate_keep, up_keep, down_keep
):
    model_block = tokens.shape[1]
    gate_used = masked(gate_weight, gate_keep)
    up_used = masked(up_weight, up_keep)
    down_used = masked(down_weight, down_keep)
    token_panel = lax.all_gather(tokens, "col", axis=0, tiled=True)
    grad_panel = lax.all_gather(grad_out, "col", axis=0, tiled=True)
    gate_part = product(token_panel, gate_used, False)
    up_part = product(token_panel, up_used, False)
    back_part = product(grad_panel, down_used, True)
    gate_sum, up_sum, back_sum = (
        lax.psum(part.astype(BF16), "row").astype(F32) for part in (gate_part, up_part, back_part)
    )
    gate_sig = jax.nn.sigmoid(gate_sum)
    hidden = (gate_sum * gate_sig * up_sum).astype(BF16)
    gate_grad, up_grad = swiglu_grads(back_sum, gate_sum, gate_sig, up_sum)
    both = lambda value: lax.all_gather(value, "rep", axis=0, tiled=True)
    tokens_all, grads_all, hidden_all, gate_all, up_all = (
        both(value) for value in (token_panel, grad_panel, hidden, gate_grad, up_grad)
    )
    over = lambda left, right, keep: masked(
        lax.dot_general(left, right, OVER_ROWS, preferred_element_type=F32), keep
    ).astype(BF16)
    forward = product(hidden, down_used, False)
    backward = product(gate_grad, gate_used, True) + product(up_grad, up_used, True)
    combined = lax.psum_scatter(
        jnp.concatenate([forward, backward], axis=1).astype(BF16),
        "col",
        scatter_dimension=0,
        tiled=True,
    )
    return (
        combined[:, :model_block],
        combined[:, model_block:],
        over(tokens_all, gate_all, gate_keep),
        over(tokens_all, up_all, up_keep),
        over(hidden_all, grads_all, down_keep),
    )


def layer_kernel(
    n, n_col,
    x_ref, dy_ref, gate_ref, up_ref, down_ref, gk_ref, uk_ref, dk_ref,
    mixed_ref, input_ref, xp_ref, yp_ref, h_ref,
    w, d, part, sums, arrived, acc_m, acc_i, parts_out, parts_in,
    load_sem, ag_send, ag_recv, hop_send, hop_recv, bc_send, bc_recv, pt_send, pt_recv,
    rs_send, rs_recv,
):
    me, c, r = lax.axis_index("row"), lax.axis_index("col"), lax.axis_index("rep")
    peers = 2 * n_col
    index = c * 2 + r
    rows = x_ref.shape[0]
    nb = w.shape[0]
    half = nb // 2
    model_blocks = x_ref.shape[1] // BLOCK

    def loads(b):
        g = r * nb + b
        cols = pl.ds(pl.multiple_of(g * BLOCK, BLOCK), BLOCK)
        return (
            pltpu.make_async_copy(gate_ref.at[:, cols], w.at[b, :, pl.ds(0, BLOCK)], load_sem.at[0, b]),
            pltpu.make_async_copy(up_ref.at[:, cols], w.at[b, :, pl.ds(BLOCK, BLOCK)], load_sem.at[1, b]),
            pltpu.make_async_copy(down_ref.at[cols], d.at[b], load_sem.at[2, b]),
        )

    def start_loads(j, carry):
        for base in (0, half):
            for copy in loads(base + j):
                copy.start()
        return carry

    barrier = pltpu.get_barrier_semaphore()
    others = [lax.rem(index + o, peers) for o in range(1, peers)]
    for other in others:
        pl.semaphore_signal(barrier, inc=1, device_id=(me, other // 2, other % 2), device_id_type=MESH)

    @pl.when(me > 0)
    def _():
        pl.semaphore_signal(barrier, inc=1, device_id=(me - 1, c, r), device_id_type=MESH)

    @pl.when(me < n - 1)
    def _():
        pl.semaphore_signal(barrier, inc=1, device_id=(me + 1, c, r), device_id_type=MESH)

    lax.fori_loop(0, half, start_loads, 0)
    edges = jnp.where(me > 0, 1, 0) + jnp.where(me < n - 1, 1, 0)
    pl.semaphore_wait(barrier, peers - 1 + edges)

    def panel(src, dst, kind, owner, target):
        return pltpu.make_async_remote_copy(
            src_ref=src,
            dst_ref=dst.at[pl.ds(pl.multiple_of(owner * rows, rows), rows)],
            send_sem=ag_send.at[kind, target],
            recv_sem=ag_recv.at[kind, owner],
            device_id=(me, target // 2, target % 2),
            device_id_type=MESH,
        )

    for other in others:
        panel(x_ref, xp_ref, 0, index, other).start()
        panel(dy_ref, yp_ref, 1, index, other).start()
    own = pl.ds(pl.multiple_of(index * rows, rows), rows)
    xp_ref[own] = x_ref[...]
    yp_ref[own] = dy_ref[...]
    acc_m[...] = jnp.zeros_like(acc_m)
    acc_i[...] = jnp.zeros_like(acc_i)
    for other in others:
        panel(x_ref, xp_ref, 0, other, other).wait_recv()
        panel(dy_ref, yp_ref, 1, other, other).wait_recv()

    def compute(b):
        for copy in loads(b):
            copy.wait()
        g = r * nb + b
        for a in range(model_blocks):
            span = pl.ds(a * BLOCK, BLOCK)
            first, second = pl.ds(0, BLOCK), pl.ds(BLOCK, BLOCK)
            w[b, span, first] = (w[b, span, first].astype(F32) * gk_ref[a, g].astype(F32)).astype(BF16)
            w[b, span, second] = (w[b, span, second].astype(F32) * uk_ref[a, g].astype(F32)).astype(BF16)
            d[b, :, span] = (d[b, :, span].astype(F32) * dk_ref[g, a].astype(F32)).astype(BF16)
        part[b, :, pl.ds(0, 2 * BLOCK)] = product(xp_ref[...], w[b], False)
        part[b, :, pl.ds(2 * BLOCK, BLOCK)] = product(yp_ref[...], d[b], True)

    def hop_copy(b, device):
        return pltpu.make_async_remote_copy(
            src_ref=sums.at[b],
            dst_ref=arrived.at[b],
            send_sem=hop_send.at[b],
            recv_sem=hop_recv.at[b],
            device_id=(device, c, r),
            device_id_type=MESH,
        )

    def cast_copy(b, device):
        g = r * nb + b
        return pltpu.make_async_remote_copy(
            src_ref=h_ref.at[g],
            dst_ref=h_ref.at[g],
            send_sem=bc_send.at[b],
            recv_sem=bc_recv.at[b],
            device_id=(device, c, r),
            device_id_type=MESH,
        )

    def pair_copy(b, rep):
        g = rep * nb + b
        return pltpu.make_async_remote_copy(
            src_ref=h_ref.at[g],
            dst_ref=h_ref.at[g],
            send_sem=pt_send.at[b],
            recv_sem=pt_recv.at[b],
            device_id=(me, c, 1 - r),
            device_id_type=MESH,
        )

    def hop(j, pos, before, after, base):
        @pl.when((j >= 0) & (j < half))
        def _():
            b = base + j

            @pl.when(pos > 0)
            def _():
                hop_copy(b, before).wait_recv()
                part[b] = part[b] + arrived[b].astype(F32)

            @pl.when(pos < n - 1)
            def _():
                sums[b] = part[b].astype(BF16)
                hop_copy(b, after).start()

            @pl.when(pos == n - 1)
            def _():
                gate_sum = part[b, :, pl.ds(0, BLOCK)]
                up_sum = part[b, :, pl.ds(BLOCK, BLOCK)]
                back_sum = part[b, :, pl.ds(2 * BLOCK, BLOCK)]
                gate_sig = jax.nn.sigmoid(gate_sum)
                gate_grad, up_grad = swiglu_grads(back_sum, gate_sum, gate_sig, up_sum)
                g = r * nb + b
                h_ref[g, :, pl.ds(0, BLOCK)] = (gate_sum * gate_sig * up_sum).astype(BF16)
                h_ref[g, :, pl.ds(BLOCK, BLOCK)] = gate_grad
                h_ref[g, :, pl.ds(2 * BLOCK, BLOCK)] = up_grad

    def cast(j, pos, before, after, base):
        @pl.when((j >= 0) & (j < half))
        def _():
            b = base + j

            @pl.when(pos < n - 1)
            def _():
                cast_copy(b, after).wait_recv()

            @pl.when(pos > 0)
            def _():
                cast_copy(b, before).start()

            pair_copy(b, r).start()

    def consume(j, base):
        @pl.when((j >= 0) & (j < half))
        def _():
            b = base + j
            g = r * nb + b
            acc_m[...] += product(h_ref[g, :, pl.ds(0, BLOCK)], d[b], False)
            acc_i[...] += product(h_ref[g, :, pl.ds(BLOCK, 2 * BLOCK)], w[b], True)

    back = n - 1 - me
    low, high = me - 1, me + 1
    ways = ((me, low, high, 0), (back, high, low, half))

    compute(0)
    compute(half)

    def step(t, carry):
        for pos, before, after, base in ways:
            hop(t - pos, pos, before, after, base)
        for pos, before, after, base in ways:
            cast(t - 2 * (n - 1) + pos, pos, before, after, base)

        @pl.when(t + 1 < half)
        def _():
            compute(t + 1)
            compute(half + t + 1)

        for pos, before, after, base in ways:
            consume(t - 2 * (n - 1) + pos, base)
        return carry

    lax.fori_loop(0, half + 2 * (n - 1), step, 0)

    for p in range(peers):
        span = pl.ds(p * rows, rows)
        parts_out[p, pl.ds(0, rows)] = acc_m[span].astype(BF16)
        parts_out[p, pl.ds(rows, rows)] = acc_i[span].astype(BF16)

    def share(owner, source):
        return pltpu.make_async_remote_copy(
            src_ref=parts_out.at[owner],
            dst_ref=parts_in.at[source],
            send_sem=rs_send.at[owner],
            recv_sem=rs_recv.at[source],
            device_id=(me, owner // 2, owner % 2),
            device_id_type=MESH,
        )

    for other in others:
        share(other, index).start()
    total = parts_out[index].astype(F32)

    def drain(b, carry):
        pair_copy(b, r).wait_send()
        pair_copy(b, 1 - r).wait_recv()
        return carry

    lax.fori_loop(0, nb, drain, 0)
    for pos, before, after, base in ways:

        @pl.when(pos < n - 1)
        def _():
            def body(j, carry):
                hop_copy(base + j, after).wait_send()
                return carry

            lax.fori_loop(0, half, body, 0)

        @pl.when(pos > 0)
        def _():
            def body(j, carry):
                cast_copy(base + j, before).wait_send()
                return carry

            lax.fori_loop(0, half, body, 0)

    for other in others:
        panel(x_ref, xp_ref, 0, index, other).wait_send()
        panel(dy_ref, yp_ref, 1, index, other).wait_send()
    for other in others:
        pltpu.make_async_remote_copy(
            src_ref=parts_out.at[other],
            dst_ref=parts_in.at[other],
            send_sem=rs_send.at[other],
            recv_sem=rs_recv.at[other],
            device_id=(me, other // 2, other % 2),
            device_id_type=MESH,
        ).wait_recv()
        total = total + parts_in[other].astype(F32)
    mixed_ref[...] = total[:rows].astype(BF16)
    input_ref[...] = total[rows:].astype(BF16)
    for other in others:
        share(other, index).wait_send()


def weight_kernel(x_ref, y_ref, h_ref, gk_ref, uk_ref, dk_ref, gate_ref, up_ref, down_ref, xt):
    s = pl.program_id(0)
    wide = h_ref.shape[0]
    model_blocks = x_ref.shape[1] // BLOCK

    @pl.when(s == 0)
    def _():
        xt[...] = x_ref[...].T

    for i in range(wide):
        g = s * wide + i
        cols = pl.ds(i * BLOCK, BLOCK)
        grads = h_ref[i, :, pl.ds(BLOCK, 2 * BLOCK)]
        hidden = h_ref[i, :, pl.ds(0, BLOCK)].T
        for a in range(model_blocks):
            span = pl.ds(a * BLOCK, BLOCK)
            term = product(xt[span], grads, False)
            gate_ref[span, cols] = (term[:, :BLOCK] * gk_ref[a, g].astype(F32)).astype(BF16)
            up_ref[span, cols] = (term[:, BLOCK:] * uk_ref[a, g].astype(F32)).astype(BF16)
            down = product(hidden, y_ref[:, span], False)
            down_ref[cols, span] = (down * dk_ref[g, a].astype(F32)).astype(BF16)


def kernel_device(
    n, n_col,
    tokens, grad_out, gate_weight, up_weight, down_weight, gate_keep, up_keep, down_keep,
):
    rows, model = tokens.shape
    hidden = gate_weight.shape[1]
    everyone = 2 * n_col * rows
    peers = 2 * n_col
    nb = hidden // (2 * BLOCK)
    vmem = pl.BlockSpec(memory_space=pltpu.VMEM)
    smem = pl.BlockSpec(memory_space=pltpu.SMEM)
    far = pl.BlockSpec(memory_space=pl.ANY)
    dma = pltpu.SemaphoreType.DMA
    mixed, input_grad, token_panel, grad_panel, hidden_blocks = pl.pallas_call(
        functools.partial(layer_kernel, n, n_col),
        out_shape=(
            jax.ShapeDtypeStruct((rows, model), BF16),
            jax.ShapeDtypeStruct((rows, model), BF16),
            jax.ShapeDtypeStruct((everyone, model), BF16),
            jax.ShapeDtypeStruct((everyone, model), BF16),
            jax.ShapeDtypeStruct((2 * nb, everyone, 3 * BLOCK), BF16),
        ),
        in_specs=[vmem, vmem, far, far, far, smem, smem, smem],
        out_specs=(vmem,) * 5,
        scratch_shapes=[
            pltpu.VMEM((nb, model, 2 * BLOCK), BF16),
            pltpu.VMEM((nb, BLOCK, model), BF16),
            pltpu.VMEM((nb, everyone, 3 * BLOCK), F32),
            pltpu.VMEM((nb, everyone, 3 * BLOCK), BF16),
            pltpu.VMEM((nb, everyone, 3 * BLOCK), BF16),
            pltpu.VMEM((everyone, model), F32),
            pltpu.VMEM((everyone, model), F32),
            pltpu.VMEM((peers, 2 * rows, model), BF16),
            pltpu.VMEM((peers, 2 * rows, model), BF16),
            dma((3, nb)),
            dma((2, peers)),
            dma((2, peers)),
            dma((nb,)),
            dma((nb,)),
            dma((nb,)),
            dma((nb,)),
            dma((nb,)),
            dma((nb,)),
            dma((peers,)),
            dma((peers,)),
        ],
        compiler_params=pltpu.CompilerParams(
            collective_id=0, has_side_effects=True, vmem_limit_bytes=56 * 1024 * 1024
        ),
        name="layer",
    )(tokens, grad_out, gate_weight, up_weight, down_weight, gate_keep, up_keep, down_keep)
    wide = 2
    whole = pl.BlockSpec((everyone, model), lambda s: (0, 0))
    gate_grad, up_grad, down_grad = pl.pallas_call(
        weight_kernel,
        grid=(2 * nb // wide,),
        out_shape=(
            jax.ShapeDtypeStruct((model, hidden), BF16),
            jax.ShapeDtypeStruct((model, hidden), BF16),
            jax.ShapeDtypeStruct((hidden, model), BF16),
        ),
        in_specs=[
            whole,
            whole,
            pl.BlockSpec((wide, everyone, 3 * BLOCK), lambda s: (s, 0, 0)),
            smem,
            smem,
            smem,
        ],
        out_specs=(
            pl.BlockSpec((model, wide * BLOCK), lambda s: (0, s)),
            pl.BlockSpec((model, wide * BLOCK), lambda s: (0, s)),
            pl.BlockSpec((wide * BLOCK, model), lambda s: (s, 0)),
        ),
        scratch_shapes=[pltpu.VMEM((model, everyone), BF16)],
        compiler_params=pltpu.CompilerParams(vmem_limit_bytes=32 * 1024 * 1024),
        name="weights",
    )(token_panel, grad_panel, hidden_blocks, gate_keep, up_keep, down_keep)
    return mixed, input_grad, gate_grad, up_grad, down_grad


def per_device(n, n_col, n_rep, *args):
    tokens, gate_weight = args[0], args[2]
    rows, model = tokens.shape
    hidden = gate_weight.shape[1]
    fits = (
        n_rep == 2
        and n > 1
        and rows % 16 == 0
        and (2 * n_col * rows) % 128 == 0
        and model % 128 == 0
        and hidden % (4 * BLOCK) == 0
    )
    if fits:
        return kernel_device(n, n_col, *args)
    return plain_device(*args)


def solution(mesh):
    shape = mesh.shape
    return jax.shard_map(
        functools.partial(per_device, shape["row"], shape["col"], shape["rep"]),
        mesh=mesh,
        in_specs=(
            P(("col", "rep"), "row"),
            P(("col", "rep"), "row"),
            P("row", "col"),
            P("row", "col"),
            P("col", "row"),
            P("row", "col"),
            P("row", "col"),
            P("col", "row"),
        ),
        out_specs=(
            P(("col", "rep"), "row"),
            P(("col", "rep"), "row"),
            P("row", "col"),
            P("row", "col"),
            P("col", "row"),
        ),
        check_vma=False,
    )
```

time: 288 us -> 93.7 us (0.33)
  waiting for transfers between devices: 143 us -> 0 us
  Pallas kernels: 0 us -> 84.4 us
  local copies, waits for them, and re-layouts: 59.5 us -> 7.8 us
  matrix products: 48.6 us -> 0 us
  blocking collectives: 18.3 us -> 0 us
  between operations: 14 us -> 0.68 us
  other arithmetic: 3.04 us -> 0 us
    psum x2 -> x0, waiting for transfers between devices: 138 us -> none  [the longest x1 74.8 us: per_device(): lax.psum(gate_term.astype(jnp.bfloat16), 'rep').astype(jnp.float32)]
    pallas_call x0 -> x2, Pallas kernels: none -> 84.4 us  [the longest x1 70.5 us: kernel_device(): pl.pallas_call(functools.partial(layer_kernel, n, n_col), out_shape=(jax....]
    dot_general x9 -> x0, matrix products: 48.6 us -> none  [the longest x6 33.4 us: product(): lax.dot_general(left, weight, FLIPPED if flipped else PLAIN, preferred_el...]
    unnamed x39 -> x15, local copies, waits for them, and re-layouts: 51.5 us -> 7.8 us
    all_gather x2 -> x0, blocking collectives: 18.3 us -> none  [the longest x1 10.1 us: per_device(): lax.all_gather(tokens, 'col', axis=0, tiled=True)]
    mul x6 -> x0, local copies, waits for them, and re-layouts: 6.05 us -> none  [masked(): tiled * keep[:, None, :, None].astype(weight.dtype)]
    reduce_scatter x1 -> x0, waiting for transfers between devices: 5.33 us -> none  [per_device(): lax.psum_scatter(jnp.concatenate([forward, backward], axis=1).astype(jnp....]
  transfers between devices with their start and end apart: 3 -> 0, of which waited for: 3 -> 0; matrix products, arithmetic and copies ran while one was open for 7% -> 0% of each run, Pallas kernels for 0% -> 0%
where the time goes in v1:
time: 93.7 us; the launch traced here: 92.9 us
  Pallas kernels  84.4 us (90%)
  local copies, waits for them, and re-layouts  7.8 us (8%)
    pallas_call x1, Pallas kernels, kernel_device(): pl.pallas_call(functools.partial(layer_kernel, n, n_col), out_shape=(jax....  70.5 us
    pallas_call x1, Pallas kernels, kernel_device(): pl.pallas_call(weight_kernel, grid=(2 * nb // wide,), out_shape=(jax.Shap...  13.9 us
    unnamed x15, local copies, waits for them, and re-layouts  7.8 us

profile of v1, /device:TPU:0, one launch (start us, length us, event | category | flops | bytes accessed | tf_op | source)
XLA Modules:
  0.0 92.9 jit_solution(8836676112829935922)
XLA Ops:
  0.6 1.4 %copy.13.dk_ref = s32[28,8]{1,0:T(8,128)} copy(s32[28,8]{0,1:T(8,128)} %param.15) | data formatting | bytes 1792 | tf_op args[7]
  2.0 0.0 copy-start.3
  2.0 0.0 copy-start.4
  2.0 0.0 copy-start.5
  2.0 70.5 %layer.1 = (bf16[16,1024]{1,0:T(8,128)(2,1)}, bf16[16,1024]{1,0:T(8,128)(2,1)}, bf16[128,1024]{1,0:T(8,128)(2,1)}, bf16[128,1024]{1,0:T(8,128)(2,1)}, bf16[28,128,384]{2,1,0:T(8,128)(2,1)}) custom-call(bf16[16,1024]{1,0:T(8,128)(2,1)} %x_ref.1, bf16[16,1024]{1,0:T(8,128)(2,1)} %dy_ref.1, bf16[1024,3584]{1,0:T(8,128)(2,1)} %gate_ref.1, ...), custom_call_target="tpu_custom_call" | custom-call | tf_op jit(solution)/shard_map/layer/pallas_call | solution.py:366
  72.5 0.0 copy-done.3
  72.6 0.0 copy-done.4
  72.6 0.0 copy-done.5
  72.6 0.0 copy-start
  72.6 1.8 %copy-done = bf16[28,128,384]{2,1,0:T(8,128)(2,1)S(1)} copy-done((bf16[28,128,384]{2,1,0:T(8,128)(2,1)S(1)}, bf16[28,128,384]{2,1,0:T(8,128)(2,1)}, u32[]{:S(2)}) %copy-start) | copy-done | bytes 2752536
  74.4 0.0 copy-start.1
  74.4 0.9 %copy-done.1 = bf16[128,1024]{1,0:T(8,128)(2,1)S(1)} copy-done((bf16[128,1024]{1,0:T(8,128)(2,1)S(1)}, bf16[128,1024]{1,0:T(8,128)(2,1)}, u32[]{:S(2)}) %copy-start.1) | copy-done | bytes 262168
  75.3 0.0 copy-start.2
  75.3 0.9 %copy-done.2 = bf16[128,1024]{1,0:T(8,128)(2,1)S(1)} copy-done((bf16[128,1024]{1,0:T(8,128)(2,1)S(1)}, bf16[128,1024]{1,0:T(8,128)(2,1)}, u32[]{:S(2)}) %copy-start.2) | copy-done | bytes 262168
  76.3 13.9 %weights.1 = (bf16[1024,3584]{1,0:T(8,128)(2,1)}, bf16[1024,3584]{1,0:T(8,128)(2,1)}, bf16[3584,1024]{1,0:T(8,128)(2,1)}) custom-call(bf16[128,1024]{1,0:T(8,128)(2,1)S(1)} %copy-done.1, bf16[128,1024]{1,0:T(8,128)(2,1)S(1)} %copy-done.2, bf16[28,128,384]{2,1,0:T(8,128)(2,1)S(1)} %copy-done, s32[8,28]{1,0:T(8,128)S(1)} %copy-done.4, s32[8,28]{1,0:T(8,128)S(1)} %copy-done.5, ...), custom_call_target="tpu_custom_call" | custom-call | tf_op jit(solution)/shard_map/weights/pallas_call | solution.py:406
  90.1 1.4 %copy.17 = bf16[16,1024]{1,0:T(8,128)(2,1)} copy(bf16[16,1024]{1,0:T(8,128)(2,1)} %get-tuple-element.26) | data formatting | bytes 65536
  91.5 1.4 %copy.18 = bf16[16,1024]{1,0:T(8,128)(2,1)} copy(bf16[16,1024]{1,0:T(8,128)(2,1)} %get-tuple-element.27) | data formatting | bytes 65536
Async XLA Ops:
  2.0 70.5 %copy-start.3 = (s32[28,8]{1,0:T(8,128)S(1)}, s32[28,8]{1,0:T(8,128)}, u32[]{:S(2)}) copy-start(s32[28,8]{1,0:T(8,128)} %copy.13.dk_ref) | copy-start | bytes 2692
  2.0 70.6 %copy-start.4 = (s32[8,28]{1,0:T(8,128)S(1)}, s32[8,28]{1,0:T(8,128)}, u32[]{:S(2)}) copy-start(s32[8,28]{1,0:T(8,128)} %gk_ref.3) | copy-start | bytes 2692
  2.0 70.6 %copy-start.5 = (s32[8,28]{1,0:T(8,128)S(1)}, s32[8,28]{1,0:T(8,128)}, u32[]{:S(2)}) copy-start(s32[8,28]{1,0:T(8,128)} %uk_ref.3) | copy-start | bytes 2692
  72.6 1.8 %copy-start = (bf16[28,128,384]{2,1,0:T(8,128)(2,1)S(1)}, bf16[28,128,384]{2,1,0:T(8,128)(2,1)}, u32[]{:S(2)}) copy-start(bf16[28,128,384]{2,1,0:T(8,128)(2,1)} %get-tuple-element.17.h_ref) | copy-start | bytes 8257540
  74.4 0.9 %copy-start.1 = (bf16[128,1024]{1,0:T(8,128)(2,1)S(1)}, bf16[128,1024]{1,0:T(8,128)(2,1)}, u32[]{:S(2)}) copy-start(bf16[128,1024]{1,0:T(8,128)(2,1)} %get-tuple-element.15.x_ref) | copy-start | bytes 786436
  75.3 0.9 %copy-start.2 = (bf16[128,1024]{1,0:T(8,128)(2,1)S(1)}, bf16[128,1024]{1,0:T(8,128)(2,1)}, u32[]{:S(2)}) copy-start(bf16[128,1024]{1,0:T(8,128)(2,1)} %get-tuple-element.16.y_ref) | copy-start | bytes 786436

commit v2 on v1

--- a/solution.py
+++ b/solution.py
@@ -12,6 +12,8 @@
 OVER_ROWS = (((0,), (0,)), ((), ()))
 MESH = pl.DeviceIdType.MESH
 BLOCK = 128
+SPLIT = 2
+LAG = 2
 F32 = jnp.float32
 BF16 = jnp.bfloat16
 
@@ -87,6 +89,7 @@
     me, c, r = lax.axis_index("row"), lax.axis_index("col"), lax.axis_index("rep")
     peers = 2 * n_col
     index = c * 2 + r
+    chunk = xp_ref.shape[0] // SPLIT
     rows = x_ref.shape[0]
     nb = w.shape[0]
     half = nb // 2
@@ -155,115 +158,125 @@
             first, second = pl.ds(0, BLOCK), pl.ds(BLOCK, BLOCK)
             w[b, span, first] = (w[b, span, first].astype(F32) * gk_ref[a, g].astype(F32)).astype(BF16)
             w[b, span, second] = (w[b, span, second].astype(F32) * uk_ref[a, g].astype(F32)).astype(BF16)
-            d[b, :, span] = (d[b, :, span].astype(F32) * dk_ref[g, a].astype(F32)).astype(BF16)
+            d[b, :, span] = (d[b, :, span].astype(F32) * dk_ref[a, g].astype(F32)).astype(BF16)
         part[b, :, pl.ds(0, 2 * BLOCK)] = product(xp_ref[...], w[b], False)
         part[b, :, pl.ds(2 * BLOCK, BLOCK)] = product(yp_ref[...], d[b], True)
 
-    def hop_copy(b, device):
+    def place(q):
+        return q // SPLIT, pl.ds(pl.multiple_of(lax.rem(q, SPLIT) * chunk, chunk), chunk)
+
+    def hop_copy(q, device):
+        b, span = place(q)
         return pltpu.make_async_remote_copy(
-            src_ref=sums.at[b],
-            dst_ref=arrived.at[b],
-            send_sem=hop_send.at[b],
-            recv_sem=hop_recv.at[b],
+            src_ref=sums.at[b, span],
+            dst_ref=arrived.at[b, span],
+            send_sem=hop_send.at[q],
+            recv_sem=hop_recv.at[q],
             device_id=(device, c, r),
             device_id_type=MESH,
         )
 
-    def cast_copy(b, device):
+    def cast_copy(q, device):
+        b, span = place(q)
         g = r * nb + b
         return pltpu.make_async_remote_copy(
-            src_ref=h_ref.at[g],
-            dst_ref=h_ref.at[g],
-            send_sem=bc_send.at[b],
-            recv_sem=bc_recv.at[b],
+            src_ref=h_ref.at[g, span],
+            dst_ref=h_ref.at[g, span],
+            send_sem=bc_send.at[q],
+            recv_sem=bc_recv.at[q],
             device_id=(device, c, r),
             device_id_type=MESH,
         )
 
-    def pair_copy(b, rep):
+    def pair_copy(q, rep):
+        b, span = place(q)
         g = rep * nb + b
         return pltpu.make_async_remote_copy(
-            src_ref=h_ref.at[g],
-            dst_ref=h_ref.at[g],
-            send_sem=pt_send.at[b],
-            recv_sem=pt_recv.at[b],
+            src_ref=h_ref.at[g, span],
+            dst_ref=h_ref.at[g, span],
+            send_sem=pt_send.at[q],
+            recv_sem=pt_recv.at[q],
             device_id=(me, c, 1 - r),
             device_id_type=MESH,
         )
 
     def hop(j, pos, before, after, base):
-        @pl.when((j >= 0) & (j < half))
+        @pl.when((j >= 0) & (j < count))
         def _():
-            b = base + j
+            q = base + j
+            b, span = place(q)
 
             @pl.when(pos > 0)
             def _():
-                hop_copy(b, before).wait_recv()
-                part[b] = part[b] + arrived[b].astype(F32)
+                hop_copy(q, before).wait_recv()
+                part[b, span] = part[b, span] + arrived[b, span].astype(F32)
 
             @pl.when(pos < n - 1)
             def _():
-                sums[b] = part[b].astype(BF16)
-                hop_copy(b, after).start()
+                sums[b, span] = part[b, span].astype(BF16)
+                hop_copy(q, after).start()
 
             @pl.when(pos == n - 1)
             def _():
-                gate_sum = part[b, :, pl.ds(0, BLOCK)]
-                up_sum = part[b, :, pl.ds(BLOCK, BLOCK)]
-                back_sum = part[b, :, pl.ds(2 * BLOCK, BLOCK)]
+                gate_sum = part[b, span, pl.ds(0, BLOCK)]
+                up_sum = part[b, span, pl.ds(BLOCK, BLOCK)]
+                back_sum = part[b, span, pl.ds(2 * BLOCK, BLOCK)]
                 gate_sig = jax.nn.sigmoid(gate_sum)
                 gate_grad, up_grad = swiglu_grads(back_sum, gate_sum, gate_sig, up_sum)
                 g = r * nb + b
-                h_ref[g, :, pl.ds(0, BLOCK)] = (gate_sum * gate_sig * up_sum).astype(BF16)
-                h_ref[g, :, pl.ds(BLOCK, BLOCK)] = gate_grad
-                h_ref[g, :, pl.ds(2 * BLOCK, BLOCK)] = up_grad
+                h_ref[g, span, pl.ds(0, BLOCK)] = (gate_sum * gate_sig * up_sum).astype(BF16)
+                h_ref[g, span, pl.ds(BLOCK, BLOCK)] = gate_grad
+                h_ref[g, span, pl.ds(2 * BLOCK, BLOCK)] = up_grad
 
     def cast(j, pos, before, after, base):
-        @pl.when((j >= 0) & (j < half))
+        @pl.when((j >= 0) & (j < count))
         def _():
-            b = base + j
+            q = base + j
+            b, span = place(q)
 
             @pl.when(pos < n - 1)
             def _():
-                cast_copy(b, after).wait_recv()
+                cast_copy(q, after).wait_recv()
 
             @pl.when(pos > 0)
             def _():
-                cast_copy(b, before).start()
-
-            pair_copy(b, r).start()
+                cast_copy(q, before).start()
+
+            pair_copy(q, r).start()
 
     def consume(j, base):
-        @pl.when((j >= 0) & (j < half))
+        @pl.when((j >= 0) & (j < count))
         def _():
-            b = base + j
+            q = base + j
+            b, span = place(q)
             g = r * nb + b
-            acc_m[...] += product(h_ref[g, :, pl.ds(0, BLOCK)], d[b], False)
-            acc_i[...] += product(h_ref[g, :, pl.ds(BLOCK, 2 * BLOCK)], w[b], True)
+            acc_m[span] += product(h_ref[g, span, pl.ds(0, BLOCK)], d[b], False)
+            acc_i[span] += product(h_ref[g, span, pl.ds(BLOCK, 2 * BLOCK)], w[b], True)
 
     back = n - 1 - me
     low, high = me - 1, me + 1
-    ways = ((me, low, high, 0), (back, high, low, half))
+    count = half * SPLIT
+    ways = ((me, low, high, 0), (back, high, low, count))
 
     compute(0)
     compute(half)
 
     def step(t, carry):
         for pos, before, after, base in ways:
-            hop(t - pos, pos, before, after, base)
+            hop(t - LAG * pos, pos, before, after, base)
         for pos, before, after, base in ways:
-            cast(t - 2 * (n - 1) + pos, pos, before, after, base)
-
-        @pl.when(t + 1 < half)
+            cast(t - LAG * (2 * (n - 1) - pos), pos, before, after, base)
+
+        @pl.when((lax.rem(t + 1, SPLIT) == 0) & (t + 1 < count))
         def _():
-            compute(t + 1)
-            compute(half + t + 1)
+            compute((t + 1) // SPLIT)
+            compute(half + (t + 1) // SPLIT)
 
         for pos, before, after, base in ways:
-            consume(t - 2 * (n - 1) + pos, base)
+            consume(t - LAG * (2 * (n - 1) - pos), base)
         return carry
 
-    lax.fori_loop(0, half + 2 * (n - 1), step, 0)
+    lax.fori_loop(0, count + LAG * 2 * (n - 1), step, 0)
 
     for p in range(peers):
         span = pl.ds(p * rows, rows)
@@ -289,7 +302,7 @@
         pair_copy(b, 1 - r).wait_recv()
         return carry
 
-    lax.fori_loop(0, nb, drain, 0)
+    lax.fori_loop(0, nb * SPLIT, drain, 0)
     for pos, before, after, base in ways:
 
         @pl.when(pos < n - 1)
@@ -298,7 +311,7 @@
                 hop_copy(base + j, after).wait_send()
                 return carry
 
-            lax.fori_loop(0, half, body, 0)
+            lax.fori_loop(0, count, body, 0)
 
         @pl.when(pos > 0)
         def _():
@@ -306,7 +319,7 @@
                 cast_copy(base + j, before).wait_send()
                 return carry
 
-            lax.fori_loop(0, half, body, 0)
+            lax.fori_loop(0, count, body, 0)
 
     for other in others:
         panel(x_ref, xp_ref, 0, index, other).wait_send()
@@ -327,27 +340,38 @@
         share(other, index).wait_send()
 
 
-def weight_kernel(x_ref, y_ref, h_ref, gk_ref, uk_ref, dk_ref, gate_ref, up_ref, down_ref, xt):
+def weight_kernel(
+    x_ref, y_ref, h_ref, m_ref, i_ref, gk_ref, uk_ref, dk_ref,
+    gate_ref, up_ref, down_ref, mixed_ref, input_ref, xt,
+):
     s = pl.program_id(0)
     wide = h_ref.shape[0]
-    model_blocks = x_ref.shape[1] // BLOCK
+    model = x_ref.shape[1]
+    tall = 2 * BLOCK if model % (2 * BLOCK) == 0 else BLOCK
 
     @pl.when(s == 0)
     def _():
         xt[...] = x_ref[...].T
+        mixed_ref[...] = m_ref[...]
+        input_ref[...] = i_ref[...]
 
     for i in range(wide):
         g = s * wide + i
         cols = pl.ds(i * BLOCK, BLOCK)
         grads = h_ref[i, :, pl.ds(BLOCK, 2 * BLOCK)]
         hidden = h_ref[i, :, pl.ds(0, BLOCK)].T
-        for a in range(model_blocks):
-            span = pl.ds(a * BLOCK, BLOCK)
-            term = product(xt[span], grads, False)
-            gate_ref[span, cols] = (term[:, :BLOCK] * gk_ref[a, g].astype(F32)).astype(BF16)
-            up_ref[span, cols] = (term[:, BLOCK:] * uk_ref[a, g].astype(F32)).astype(BF16)
-            down = product(hidden, y_ref[:, span], False)
-            down_ref[cols, span] = (down * dk_ref[g, a].astype(F32)).astype(BF16)
+        for begin in range(0, model, tall):
+            term = product(xt[pl.ds(begin, tall)], grads, False)
+            down = product(hidden, y_ref[:, pl.ds(begin, tall)], False)
+            for inner in range(0, tall, BLOCK):
+                a = (begin + inner) // BLOCK
+                span = pl.ds(begin + inner, BLOCK)
+                part = term[inner : inner + BLOCK]
+                gate_ref[span, cols] = (part[:, :BLOCK] * gk_ref[a, g].astype(F32)).astype(BF16)
+                up_ref[span, cols] = (part[:, BLOCK:] * uk_ref[a, g].astype(F32)).astype(BF16)
+                down_ref[cols, span] = (
+                    down[:, inner : inner + BLOCK] * dk_ref[a, g].astype(F32)
+                ).astype(BF16)
 
 
 def kernel_device(
@@ -355,6 +379,7 @@
     tokens, grad_out, gate_weight, up_weight, down_weight, gate_keep, up_keep, down_keep,
 ):
     rows, model = tokens.shape
+    down_keep = down_keep.T
     hidden = gate_weight.shape[1]
     everyone = 2 * n_col * rows
     peers = 2 * n_col
@@ -387,12 +412,12 @@
             dma((3, nb)),
             dma((2, peers)),
             dma((2, peers)),
-            dma((nb,)),
-            dma((nb,)),
-            dma((nb,)),
-            dma((nb,)),
-            dma((nb,)),
-            dma((nb,)),
+            dma((nb * SPLIT,)),
+            dma((nb * SPLIT,)),
+            dma((nb * SPLIT,)),
+            dma((nb * SPLIT,)),
+            dma((nb * SPLIT,)),
+            dma((nb * SPLIT,)),
             dma((peers,)),
             dma((peers,)),
         ],
@@ -403,18 +428,23 @@
     )(tokens, grad_out, gate_weight, up_weight, down_weight, gate_keep, up_keep, down_keep)
     wide = 2
     whole = pl.BlockSpec((everyone, model), lambda s: (0, 0))
-    gate_grad, up_grad, down_grad = pl.pallas_call(
+    small = pl.BlockSpec((rows, model), lambda s: (0, 0))
+    gate_grad, up_grad, down_grad, mixed, input_grad = pl.pallas_call(
         weight_kernel,
         grid=(2 * nb // wide,),
         out_shape=(
             jax.ShapeDtypeStruct((model, hidden), BF16),
             jax.ShapeDtypeStruct((model, hidden), BF16),
             jax.ShapeDtypeStruct((hidden, model), BF16),
+            jax.ShapeDtypeStruct((rows, model), BF16),
+            jax.ShapeDtypeStruct((rows, model), BF16),
         ),
         in_specs=[
             whole,
             whole,
             pl.BlockSpec((wide, everyone, 3 * BLOCK), lambda s: (s, 0, 0)),
+            small,
+            small,
             smem,
             smem,
             smem,
@@ -423,11 +453,13 @@
             pl.BlockSpec((model, wide * BLOCK), lambda s: (0, s)),
             pl.BlockSpec((model, wide * BLOCK), lambda s: (0, s)),
             pl.BlockSpec((wide * BLOCK, model), lambda s: (s, 0)),
+            small,
+            small,
         ),
         scratch_shapes=[pltpu.VMEM((model, everyone), BF16)],
-        compiler_params=pltpu.CompilerParams(vmem_limit_bytes=32 * 1024 * 1024),
+        compiler_params=pltpu.CompilerParams(vmem_limit_bytes=60 * 1024 * 1024),
         name="weights",
-    )(token_panel, grad_panel, hidden_blocks, gate_keep, up_keep, down_keep)
+    )(token_panel, grad_panel, hidden_blocks, mixed, input_grad, gate_keep, up_keep, down_keep)
     return mixed, input_grad, gate_grad, up_grad, down_grad
 
 
@@ -439,7 +471,7 @@
         n_rep == 2
         and n > 1
         and rows % 16 == 0
-        and (2 * n_col * rows) % 128 == 0
+        and (2 * n_col * rows) % (64 * SPLIT) == 0
         and model % 128 == 0
         and hidden % (4 * BLOCK) == 0
     )

time: 93.7 us -> 84.7 us (0.904)
  local copies, waits for them, and re-layouts: 7.8 us -> 0 us
  Pallas kernels: 84.4 us -> 83.4 us
    unnamed x15 -> x0, local copies, waits for them, and re-layouts: 7.8 us -> none
    pallas_call x1, Pallas kernels: 70.5 us -> 68.2 us  [kernel_device(): pl.pallas_call(functools.partial(layer_kernel, n, n_col), out_shape=(jax....]
    pallas_call x1, Pallas kernels: 13.9 us -> 15.2 us  [kernel_device(): pl.pallas_call(weight_kernel, grid=(2 * nb // wide,), out_shape=(jax.Shap...]
where the time goes in v2:
time: 84.7 us; the launch traced here: 84.1 us
  Pallas kernels  83.4 us (98%)
    pallas_call x1, Pallas kernels, kernel_device(): pl.pallas_call(functools.partial(layer_kernel, n, n_col), out_shape=(jax....  68.2 us
    pallas_call x1, Pallas kernels, kernel_device(): pl.pallas_call(weight_kernel, grid=(2 * nb // wide,), out_shape=(jax.Shap...  15.2 us

profile of v2, /device:TPU:0, one launch (start us, length us, event | category | flops | bytes accessed | tf_op | source)
XLA Modules:
  0.0 84.1 jit_solution(448071906298182352)
XLA Ops:
  0.6 68.2 %layer.1 = (bf16[16,1024]{1,0:T(8,128)(2,1)}, bf16[16,1024]{1,0:T(8,128)(2,1)}, bf16[128,1024]{1,0:T(8,128)(2,1)}, bf16[128,1024]{1,0:T(8,128)(2,1)}, bf16[28,128,384]{2,1,0:T(8,128)(2,1)}) custom-call(bf16[16,1024]{1,0:T(8,128)(2,1)} %x_ref.1, bf16[16,1024]{1,0:T(8,128)(2,1)} %dy_ref.1, bf16[1024,3584]{1,0:T(8,128)(2,1)} %gate_ref.1, ...), custom_call_target="tpu_custom_call" | custom-call | tf_op jit(solution)/shard_map/layer/pallas_call | solution.py:391
  68.9 15.2 %weights.1 = (bf16[1024,3584]{1,0:T(8,128)(2,1)}, bf16[1024,3584]{1,0:T(8,128)(2,1)}, bf16[3584,1024]{1,0:T(8,128)(2,1)}, bf16[16,1024]{1,0:T(8,128)(2,1)}, bf16[16,1024]{1,0:T(8,128)(2,1)}) custom-call(bf16[128,1024]{1,0:T(8,128)(2,1)} %get-tuple-element.15.x_ref, bf16[128,1024]{1,0:T(8,128)(2,1)} %get-tuple-element.16.y_ref, ...), custom_call_target="tpu_custom_call" | custom-call | tf_op jit(solution)/shard_map/weights/pallas_call | solution.py:432
